TPU v7x, 32 devices: a whole 2x2x4 slice. The times are simulated.
32 devices in a mesh: row: 4 (over z), col: 8 (over y, x, core).
Axes of the slice: x: 2, y: 2, z: 4, core: 2. Of those that a mesh axis runs over, the one named last changes fastest.
Arguments:
- patches: bfloat16 [8, 16, 32, 768], P('col', 'row'), may hold values from -6 to 6
- pixel_grads: bfloat16 [8, 16, 32, 768], P('col', 'row'), may hold values from -6 to 6
- widths: int32 [8], P('col'), may hold values from 8 to 32, as said below
- patch_mask: int32 [8, 16, 32], P('col'), may hold values from 0 to 1, as said below
- heads_weight: float32 [768, 2304], P('col'), may hold values from -0.21875 to 0.21875
- heads_first: float32 [768, 2304], P('col'), may hold values from -192 to 192
- heads_second: float32 [768, 2304], P('col'), may hold values from 1024 to 4096
- merge_weight: float32 [768, 768], P('col'), may hold values from -1.75 to 1.75
- merge_first: float32 [768, 768], P('col'), may hold values from -96 to 96
- merge_second: float32 [768, 768], P('col'), may hold values from 256 to 1024
- expand_weight: float32 [768, 3072], P('col'), may hold values from -0.21875 to 0.21875
- expand_first: float32 [768, 3072], P('col'), may hold values from -96 to 96
- expand_second: float32 [768, 3072], P('col'), may hold values from 256 to 1024
- shrink_weight: float32 [3072, 768], P('col'), may hold values from -0.109375 to 0.109375
- shrink_first: float32 [3072, 768], P('col'), may hold values from -192 to 192
- shrink_second: float32 [3072, 768], P('col'), may hold values from 1024 to 4096
- kernel_weight: float32 [9, 768, 768], P(None, 'col'), may hold values from -0.078125 to 0.078125
- kernel_first: float32 [9, 768, 768], P(None, 'col'), may hold values from -256 to 256
- kernel_second: float32 [9, 768, 768], P(None, 'col'), may hold values from 2048 to 8192
- norm_table: float32 [4, 768], P(None, 'col'), may hold values from -1 to 2, as said below
- norm_first: float32 [4, 768], P(None, 'col'), may hold values from -384 to 384
- norm_second: float32 [4, 768], P(None, 'col'), may hold values from 4096 to 16384
Outputs:
- pixels: bfloat16 [8, 16, 32, 768], P('col', 'row')
- patch_gradient: float32 [8, 16, 32, 768], P('col', 'row')
- heads_gradient: float32 [768, 2304], P('col')
- heads_mean: float32 [768, 2304], P('col')
- heads_square: float32 [768, 2304], P('col')
- heads_master: float32 [768, 2304], P('col')
- heads_copy: bfloat16 [768, 2304], P('col')
- merge_gradient: float32 [768, 768], P('col')
- merge_mean: float32 [768, 768], P('col')
- merge_square: float32 [768, 768], P('col')
- merge_master: float32 [768, 768], P('col')
- merge_copy: bfloat16 [768, 768], P('col')
- expand_gradient: float32 [768, 3072], P('col')
- expand_mean: float32 [768, 3072], P('col')
- expand_square: float32 [768, 3072], P('col')
- expand_master: float32 [768, 3072], P('col')
- expand_copy: bfloat16 [768, 3072], P('col')
- shrink_gradient: float32 [3072, 768], P('col')
- shrink_mean: float32 [3072, 768], P('col')
- shrink_square: float32 [3072, 768], P('col')
- shrink_master: float32 [3072, 768], P('col')
- shrink_copy: bfloat16 [3072, 768], P('col')
- kernel_gradient: float32 [9, 768, 768], P(None, 'col')
- kernel_mean: float32 [9, 768, 768], P(None, 'col')
- kernel_square: float32 [9, 768, 768], P(None, 'col')
- kernel_master: float32 [9, 768, 768], P(None, 'col')
- kernel_copy: bfloat16 [9, 768, 768], P(None, 'col')
- norm_gradient: float32 [4, 768], P(None, 'col')
- norm_mean: float32 [4, 768], P(None, 'col')
- norm_square: float32 [4, 768], P(None, 'col')
- norm_master: float32 [4, 768], P(None, 'col')
- norm_copy: bfloat16 [4, 768], P(None, 'col')
Inputs may be any that keep to these rules, and one draw needn't show every extreme that they name: Grid widths lie from 8 to 32; in every draw some image has 32 columns and another 32 // 4. `patch_mask`: the first slot (row 0, column 0) of every image is 1. `norm_table`: rows 0 and 2 are gains within 0.7 to 1.3, rows 1 and 3 shifts within -0.9 to 0.9.
All inputs are finite; a program needn't handle non-finite values.
Results may differ from a plain program's by a relative error of at most 0.012.
The roundings to bfloat16 on the way count: a program that leaves them out, or rounds other values in their place, can miss the bound.
Values may be sent and summed in bfloat16 or wider, within the bound.
A program may use at most 256 MiB of HBM per device.

v0:
```python
import jax
import jax.numpy as jnp
from jax import lax
from jax.sharding import PartitionSpec as P

D = 768
HEADS = 12
HEAD_DIM = 64
FF = 3072
STEP = 5


beta_first = 0.5
beta_second = 0.5


def padded(cells, sides, width):
    for axis, dim in sides:
        count = lax.axis_size(axis)
        ends = count - 1
        head = lax.slice_in_dim(cells, 0, width, axis=dim)
        tail = lax.slice_in_dim(cells, cells.shape[dim] - width, cells.shape[dim], axis=dim)
        cells = jnp.concatenate(
            [
                lax.ppermute(tail, axis, [(i, (i + 1) % count) for i in range(ends)]),
                cells,
                lax.ppermute(head, axis, [((i + 1) % count, i) for i in range(ends)]),
            ],
            axis=dim,
        )
    return cells


def layer_norm(values, norm_gain, norm_shift):
    center = values - jnp.mean(values, axis=-1, keepdims=True)
    spread = jnp.mean(center * center, axis=-1, keepdims=True)
    return center * lax.rsqrt(spread + 1e-05) * norm_gain + norm_shift


def exact_gelu(values):
    return jax.nn.gelu(values, approximate=False)


def valid_cells(widths, patch_mask):
    column = jnp.arange(patch_mask.shape[-1], dtype=jnp.int32)
    inside = column[None, None, :] < widths[:, None, None]
    return jnp.logical_and(inside, patch_mask == 1)


def step_rates():
    return (D ** (-0.5), 8.0 * D ** (-0.5), D ** (-0.5), FF ** (-0.5), (9 * D) ** (-0.5), 0.3)


def adam_update(master, moment_one, moment_two, gradient, step_rate):
    new_mean = beta_first * moment_one + (1.0 - beta_first) * gradient
    new_square = beta_second * moment_two + (1.0 - beta_second) * gradient * gradient
    mean_hat = new_mean / (1.0 - beta_first**STEP)
    square_hat = new_square / (1.0 - beta_second**STEP)
    new_master = master - step_rate * (mean_hat / (jnp.sqrt(square_hat) + 1e-08) + 0.01 * master)
    return (gradient, new_mean, new_square, new_master, new_master.astype(jnp.bfloat16))


def per_device(
    patches,
    pixel_grads,
    widths,
    patch_mask,
    heads_weight,
    heads_first,
    heads_second,
    merge_weight,
    merge_first,
    merge_second,
    expand_weight,
    expand_first,
    expand_second,
    shrink_weight,
    shrink_first,
    shrink_second,
    kernel_weight,
    kernel_first,
    kernel_second,
    norm_table,
    norm_first,
    norm_second,
):
    images, rows_here, cols_here, model_width = patches.shape
    length = rows_here * cols_here
    heads_full, merge_full, expand_full, shrink_full, kernel_full, norm_full = (
        lax.all_gather(heads_weight.astype(jnp.bfloat16), "col", axis=0, tiled=True),
        lax.all_gather(merge_weight.astype(jnp.bfloat16), "col", axis=0, tiled=True),
        lax.all_gather(expand_weight.astype(jnp.bfloat16), "col", axis=0, tiled=True),
        lax.all_gather(shrink_weight.astype(jnp.bfloat16), "col", axis=0, tiled=True),
        lax.all_gather(kernel_weight.astype(jnp.bfloat16), "col", axis=1, tiled=True),
        lax.all_gather(norm_table.astype(jnp.bfloat16), "col", axis=1, tiled=True),
    )
    usable_all = valid_cells(widths, patch_mask)
    usable = lax.dynamic_slice_in_dim(usable_all, lax.axis_index("row") * rows_here, rows_here, 1)
    key_valid = usable_all.reshape(images, -1)
    gains = norm_full.astype(jnp.float32)
    tokens = patches.reshape(images, length, model_width).astype(jnp.float32)
    normed = layer_norm(tokens, gains[0], gains[1]).astype(jnp.bfloat16)
    projected = jnp.einsum(
        "ntc,cj->ntj", normed, heads_full, preferred_element_type=jnp.float32
    ).astype(jnp.bfloat16)
    query_part = projected[:, :, :model_width]
    key_part = projected[:, :, model_width : 2 * model_width]
    value_part = projected[:, :, 2 * model_width :]
    key_all, value_all = (
        lax.all_gather(key_part, "row", axis=1, tiled=True),
        lax.all_gather(value_part, "row", axis=1, tiled=True),
    )
    query_heads = query_part.reshape(images, length, HEADS, HEAD_DIM)
    key_heads = key_all.reshape(images, -1, HEADS, HEAD_DIM)
    value_heads = value_all.reshape(images, -1, HEADS, HEAD_DIM)
    scores = 0.125 * jnp.einsum(
        "nqhd,nkhd->nhqk", query_heads, key_heads, preferred_element_type=jnp.float32
    )
    scores = jnp.where(key_valid[:, None, None, :], scores, -1e30)
    row_peak = jnp.max(scores, axis=-1, keepdims=True)
    shifted_exp = jnp.exp(scores - row_peak)
    summed = jnp.sum(shifted_exp, axis=-1, keepdims=True)
    log_total = row_peak + jnp.log(summed)
    weights_low = (shifted_exp / summed).astype(jnp.bfloat16)
    attended = jnp.einsum(
        "nhqk,nkhd->nqhd", weights_low, value_heads, preferred_element_type=jnp.float32
    )
    attended = attended.astype(jnp.bfloat16).reshape(images, length, model_width)
    after_attend = tokens + jnp.einsum(
        "ntc,cd->ntd", attended, merge_full, preferred_element_type=jnp.float32
    )
    normed_two = layer_norm(after_attend, gains[2], gains[3]).astype(jnp.bfloat16)
    hidden = jnp.einsum("ntc,cf->ntf", normed_two, expand_full, preferred_element_type=jnp.float32)
    active = exact_gelu(hidden).astype(jnp.bfloat16)
    after_feed = after_attend + jnp.einsum(
        "ntf,fd->ntd", active, shrink_full, preferred_element_type=jnp.float32
    )
    cell_values = after_feed.astype(jnp.bfloat16).reshape(images, rows_here, cols_here, model_width)
    cell_values = jnp.where(usable[..., None], cell_values, jnp.zeros((), jnp.bfloat16))
    cells_rimmed = padded(cell_values, (("row", 1),), 1)
    cell_padded = jnp.pad(cells_rimmed, ((0, 0), (0, 0), (1, 1), (0, 0)))
    pixel_sum = jnp.zeros(cell_values.shape, jnp.float32)
    for kernel_tap in range(9):
        row_step = kernel_tap // 3
        col_step = kernel_tap % 3
        window = cell_padded[:, row_step : row_step + rows_here, col_step : col_step + cols_here]
        pixel_sum = pixel_sum + jnp.einsum(
            "nyxc,cd->nyxd", window, kernel_full[kernel_tap], preferred_element_type=jnp.float32
        )
    pixels = pixel_sum.astype(jnp.bfloat16)
    grads_rimmed = padded(pixel_grads, (("row", 1),), 1)
    grads_padded = jnp.pad(grads_rimmed, ((0, 0), (0, 0), (1, 1), (0, 0)))
    kernel_taps = []
    cell_grad = jnp.zeros(cell_values.shape, jnp.float32)
    for kernel_tap in range(9):
        row_step = kernel_tap // 3
        col_step = kernel_tap % 3
        window = cell_padded[:, row_step : row_step + rows_here, col_step : col_step + cols_here]
        kernel_taps.append(
            jnp.einsum("nyxc,nyxd->cd", window, pixel_grads, preferred_element_type=jnp.float32)
        )
        mirror = grads_padded[
            :, 2 - row_step : 2 - row_step + rows_here, 2 - col_step : 2 - col_step + cols_here
        ]
        cell_grad = cell_grad + jnp.einsum(
            "nyxd,cd->nyxc", mirror, kernel_full[kernel_tap], preferred_element_type=jnp.float32
        )
    kernel_grad = jnp.stack(kernel_taps)
    feed_grad = jnp.where(usable[..., None], cell_grad, 0.0).reshape(images, length, model_width)
    down_in = feed_grad.astype(jnp.bfloat16)
    shrink_grad = jnp.einsum("ntf,ntd->fd", active, down_in, preferred_element_type=jnp.float32)
    active_grad = jnp.einsum(
        "ntd,fd->ntf", down_in, shrink_full, preferred_element_type=jnp.float32
    )
    _, gelu_pull = jax.vjp(exact_gelu, hidden)
    hidden_grad = gelu_pull(active_grad)[0].astype(jnp.bfloat16)
    expand_grad = jnp.einsum(
        "ntc,ntf->cf", normed_two, hidden_grad, preferred_element_type=jnp.float32
    )
    normed_two_grad = jnp.einsum(
        "ntf,cf->ntc", hidden_grad, expand_full, preferred_element_type=jnp.float32
    )
    _, norm_pull_two = jax.vjp(layer_norm, after_attend, gains[2], gains[3])
    attend_part, gain_two_grad, shift_two_grad = norm_pull_two(normed_two_grad)
    attend_grad = feed_grad + attend_part
    branch_in = attend_grad.astype(jnp.bfloat16)
    merge_grad = jnp.einsum("ntc,ntd->cd", attended, branch_in, preferred_element_type=jnp.float32)
    attended_flat = jnp.einsum(
        "ntd,cd->ntc", branch_in, merge_full, preferred_element_type=jnp.float32
    ).astype(jnp.bfloat16)
    attended_grad = attended_flat.reshape(images, length, HEADS, HEAD_DIM)
    scores_again = 0.125 * jnp.einsum(
        "nqhd,nkhd->nhqk", query_heads, key_heads, preferred_element_type=jnp.float32
    )
    scores_again = jnp.where(key_valid[:, None, None, :], scores_again, -1e30)
    weights_again = jnp.exp(scores_again - log_total)
    prob_grad = jnp.einsum(
        "nqhd,nkhd->nhqk", attended_grad, value_heads, preferred_element_type=jnp.float32
    )
    inner_sum = jnp.sum(weights_again * prob_grad, axis=-1, keepdims=True)
    score_grad = (weights_again * (prob_grad - inner_sum)).astype(jnp.bfloat16)
    query_grad = 0.125 * jnp.einsum(
        "nhqk,nkhd->nqhd", score_grad, key_heads, preferred_element_type=jnp.float32
    )
    key_terms = 0.125 * jnp.einsum(
        "nhqk,nqhd->nkhd", score_grad, query_heads, preferred_element_type=jnp.float32
    )
    value_terms = jnp.einsum(
        "nhqk,nqhd->nkhd",
        weights_again.astype(jnp.bfloat16),
        attended_grad,
        preferred_element_type=jnp.float32,
    )
    key_grad, value_grad = (
        lax.psum_scatter(
            key_terms.reshape(images, -1, model_width), "row", scatter_dimension=1, tiled=True
        ),
        lax.psum_scatter(
            value_terms.reshape(images, -1, model_width), "row", scatter_dimension=1, tiled=True
        ),
    )
    projected_grad = jnp.concatenate(
        [query_grad.reshape(images, length, model_width), key_grad, value_grad], axis=-1
    ).astype(jnp.bfloat16)
    heads_grad = jnp.einsum(
        "ntc,ntj->cj", normed, projected_grad, preferred_element_type=jnp.float32
    )
    normed_grad = jnp.einsum(
        "ntj,cj->ntc", projected_grad, heads_full, preferred_element_type=jnp.float32
    )
    _, norm_pull_one = jax.vjp(layer_norm, tokens, gains[0], gains[1])
    token_part, gain_one_grad, shift_one_grad = norm_pull_one(normed_grad)
    patch_gradient = (attend_grad + token_part).reshape(images, rows_here, cols_here, model_width)
    norm_grad = jnp.stack([gain_one_grad, shift_one_grad, gain_two_grad, shift_two_grad])
    partial_shares = (
        lax.psum_scatter(heads_grad, "col", scatter_dimension=0, tiled=True),
        lax.psum_scatter(merge_grad, "col", scatter_dimension=0, tiled=True),
        lax.psum_scatter(expand_grad, "col", scatter_dimension=0, tiled=True),
        lax.psum_scatter(shrink_grad, "col", scatter_dimension=0, tiled=True),
        lax.psum_scatter(kernel_grad, "col", scatter_dimension=1, tiled=True),
        lax.psum_scatter(norm_grad, "col", scatter_dimension=1, tiled=True),
    )
    shares = lax.psum(
        (
            partial_shares[0],
            partial_shares[1],
            partial_shares[2],
            partial_shares[3],
            partial_shares[4],
            partial_shares[5],
        ),
        "row",
    )
    rates = step_rates()
    heads_out = adam_update(heads_weight, heads_first, heads_second, shares[0], rates[0])
    merge_out = adam_update(merge_weight, merge_first, merge_second, shares[1], rates[1])
    expand_out = adam_update(expand_weight, expand_first, expand_second, shares[2], rates[2])
    shrink_out = adam_update(shrink_weight, shrink_first, shrink_second, shares[3], rates[3])
    kernel_out = adam_update(kernel_weight, kernel_first, kernel_second, shares[4], rates[4])
    norm_out = adam_update(norm_table, norm_first, norm_second, shares[5], rates[5])
    return (
        pixels,
        patch_gradient,
        heads_out[0],
        heads_out[1],
        heads_out[2],
        heads_out[3],
        heads_out[4],
        merge_out[0],
        merge_out[1],
        merge_out[2],
        merge_out[3],
        merge_out[4],
        expand_out[0],
        expand_out[1],
        expand_out[2],
        expand_out[3],
        expand_out[4],
        shrink_out[0],
        shrink_out[1],
        shrink_out[2],
        shrink_out[3],
        shrink_out[4],
        kernel_out[0],
        kernel_out[1],
        kernel_out[2],
        kernel_out[3],
        kernel_out[4],
        norm_out[0],
        norm_out[1],
        norm_out[2],
        norm_out[3],
        norm_out[4],
    )


def solution(mesh):
    placed = (
        P("col", "row", None, None),
        P("col", "row", None, None),
        P("col"),
        P("col", None, None),
        P("col", None),
        P("col", None),
        P("col", None),
        P("col", None),
        P("col", None),
        P("col", None),
        P("col", None),
        P("col", None),
        P("col", None),
        P("col", None),
        P("col", None),
        P("col", None),
        P(None, "col", None),
        P(None, "col", None),
        P(None, "col", None),
        P(None, "col"),
        P(None, "col"),
        P(None, "col"),
    )
    return jax.shard_map(
        per_device,
        mesh=mesh,
        in_specs=placed,
        out_specs=(
            P("col", "row", None, None),
            P("col", "row", None, None),
            P("col", None),
            P("col", None),
            P("col", None),
            P("col", None),
            P("col", None),
            P("col", None),
            P("col", None),
            P("col", None),
            P("col", None),
            P("col", None),
            P("col", None),
            P("col", None),
            P("col", None),
            P("col", None),
            P("col", None),
            P("col", None),
            P("col", None),
            P("col", None),
            P("col", None),
            P("col", None),
            P(None, "col", None),
            P(None, "col", None),
            P(None, "col", None),
            P(None, "col", None),
            P(None, "col", None),
            P(None, "col"),
            P(None, "col"),
            P(None, "col"),
            P(None, "col"),
            P(None, "col"),
        ),
        check_vma=False,
    )
```

profile of v0, /device:TPU:0, one launch (start us, length us, event | category | flops | bytes accessed | tf_op | source)
XLA Modules:
  0.0 1024.0 jit_solution(5931907894551327497)
XLA Ops:
  13.8 5.1 collective-permute-start.2
  22.0 8.9 all-gather
  33.5 13.8 %all-gather.7.cloned.1.call-done = bf16[768,2304]{1,0:T(8,128)(2,1)} async-done(((bf16[96,2304]{1,0:T(8,128)(2,1)}), bf16[768,2304]{1,0:T(8,128)(2,1)}) %all-gather.7.cloned.1.call-update) | async-done | bytes 3538960 | tf_op jit(solution)/shard_map/all_gather | solution.py:90
  47.2 2.6 fusion
  50.8 19.5 %all_gather.27 = bf16[1,512,768]{2,1,0:T(8,128)(2,1)S(1)} all-gather(bf16[1,128,768]{2,1,0:T(8,128)(2,1)S(1)} %get-tuple-element.75), channel_id=1, replica_groups=mesh['row'=4,'col'=8] {'row'}, dimensions={1}, use_global_device_ids=true | all-gather | bytes 983040 | tf_op jit(solution)/shard_map/all_gather | solution.py:110
  71.5 18.1 %all_gather.26 = bf16[1,512,768]{2,1,0:T(8,128)(2,1)S(1)} all-gather(bf16[1,128,768]{2,1,0:T(8,128)(2,1)S(1)} %get-tuple-element.77), channel_id=1, replica_groups=mesh['row'=4,'col'=8] {'row'}, dimensions={1}, use_global_device_ids=true | all-gather | bytes 983040 | tf_op jit(solution)/shard_map/all_gather | solution.py:111
  99.0 16.2 %all-gather.11.cloned.1.call-done = bf16[768,3072]{1,0:T(8,128)(2,1)} async-done(((bf16[96,3072]{1,0:T(8,128)(2,1)}), bf16[768,3072]{1,0:T(8,128)(2,1)}) %all-gather.11.cloned.1.call-update) | async-done | bytes 4718608 | tf_op jit(solution)/shard_map/all_gather | solution.py:92
  115.2 4.4 fusion.78
  119.6 61.8 %all-gather.15.cloned.1.call-done = bf16[9,768,768]{2,1,0:T(8,128)(2,1)} async-done(((bf16[9,96,768]{2,1,0:T(8,128)(2,1)}), bf16[9,768,768]{2,1,0:T(8,128)(2,1)}) %all-gather.15.cloned.1.call-update) | async-done | bytes 10616848 | tf_op jit(solution)/shard_map/all_gather | solution.py:94
  199.6 23.1 %all-gather.13.cloned.1.call-done = bf16[3072,768]{1,0:T(8,128)(2,1)} async-done(((bf16[384,768]{1,0:T(8,128)(2,1)}), bf16[3072,768]{1,0:T(8,128)(2,1)}) %all-gather.13.cloned.1.call-update) | async-done | bytes 4718608 | tf_op jit(solution)/shard_map/all_gather | solution.py:93
  222.7 8.5 add_convert_fusion
  231.2 5.0 multiply_reduce_fusion.1
  240.4 2.8 fusion.5
  253.6 25.2 %reduce-scatter.13.cloned.1.call-done = f32[1,128,768]{1,2,0:T(8,128)} async-done(((f32[1,512,768]{1,2,0:T(8,128)}), f32[1,128,768]{1,2,0:T(8,128)}) %reduce-scatter.13.cloned.1.call-update) | async-done | bytes 393232 | tf_op jit(solution)/shard_map/reduce_scatter | solution.py:218
  279.8 35.6 %reduce-scatter.11.cloned.1.call-done = f32[1,128,768]{1,2,0:T(8,128)} async-done(((f32[1,512,768]{1,2,0:T(8,128)}), f32[1,128,768]{1,2,0:T(8,128)}) %reduce-scatter.11.cloned.1.call-update) | async-done | bytes 393232 | tf_op jit(solution)/shard_map/reduce_scatter | solution.py:215
  316.4 3.9 fusion.34
  321.4 5.1 fusion.77
  329.8 5.1 fusion.99
  335.7 3.2 broadcast_select_fusion
  343.0 4.3 collective-permute-done.1
  365.9 3.4 multiply_reduce_fusion.3
  370.9 59.3 %reduce-scatter.15.cloned.1.call-done = f32[96,2304]{1,0:T(8,128)} async-done(((f32[768,2304]{1,0:T(8,128)}), f32[96,2304]{1,0:T(8,128)}) %reduce-scatter.15.cloned.1.call-update) | async-done | bytes 884752 | tf_op jit(solution)/shard_map/reduce_scatter | solution.py:236
  430.2 79.9 %reduce-scatter.19.cloned.1.call-done = f32[96,3072]{1,0:T(8,128)} async-done(((f32[768,3072]{1,0:T(8,128)}), f32[96,3072]{1,0:T(8,128)}) %reduce-scatter.19.cloned.1.call-update) | async-done | bytes 1179664 | tf_op jit(solution)/shard_map/reduce_scatter | solution.py:238
  510.0 80.0 %reduce-scatter.21.cloned.1.call-done = f32[384,768]{1,0:T(8,128)} async-done(((f32[3072,768]{1,0:T(8,128)}), f32[384,768]{1,0:T(8,128)}) %reduce-scatter.21.cloned.1.call-update) | async-done | bytes 1179664 | tf_op jit(solution)/shard_map/reduce_scatter | solution.py:239
  590.1 140.7 %reduce-scatter.23.cloned.1.call-done = f32[9,96,768]{2,1,0:T(8,128)} async-done(((f32[9,768,768]{2,1,0:T(8,128)}), f32[9,96,768]{2,1,0:T(8,128)}) %reduce-scatter.23.cloned.1.call-update) | async-done | bytes 2654224 | tf_op jit(solution)/shard_map/reduce_scatter | solution.py:240
  747.0 21.2 %reduce-scatter.25.cloned.1.call-done = f32[96,4]{1,0:T(8,128)} async-done(((f32[768,4]{1,0:T(8,128)}), f32[96,4]{1,0:T(8,128)}) %reduce-scatter.25.cloned.1.call-update) | async-done | bytes 1552
  769.1 11.9 %psum.47 = f32[4,96]{1,0:T(4,128)S(1)} all-reduce(f32[4,96]{1,0:T(4,128)S(1)} %copy.78), channel_id=1, replica_groups=mesh['row'=4,'col'=8] {'row'}, use_global_device_ids=true, to_apply=%region_28.29 | all-reduce | flops 384 | bytes 3072 | tf_op jit(solution)/shard_map/psum | solution.py:243
  781.6 210.3 %all-reduce.5.cloned.1.call-done = (f32[96,2304]{1,0:T(8,128)}, f32[96,768]{1,0:T(8,128)}, f32[96,3072]{1,0:T(8,128)}, f32[384,768]{1,0:T(8,128)}, f32[9,96,768]{2,1,0:T(8,128)}) async-done(((f32[96,2304]{1,0:T(8,128)}, f32[96,768]{1,0:T(8,128)}, f32[96,3072]{1,0:T(8,128)}, f32[384,768]{1,0:T(8,128)}, f32[9,96,768]{2,1,0:T(8,128)}), (f32[96,2304]{1,0:T(8,128)}, f32[96,768]{1,0:T(8,128)}, ...) | async-done | bytes 6193168 | tf_op jit(solution)/shard_map/psum | solution.py:243
  994.1 3.4 fusion.89
  997.6 2.6 fusion.85
  1001.4 2.6 fusion.83
  1006.3 5.3 fusion.81
  (300 shorter events, 115.4 us)
Async XLA Ops:
  7.2 40.0 %all-gather.7.cloned.1.call-start = ((), (), s32[]{:S(2)}) async-start(), calls=%async_computation.8 | async-start | bytes 3981312 | tf_op jit(solution)/shard_map/all_gather | solution.py:90
  9.3 86.8 %all-gather.9.cloned.1.call-start = ((), (), s32[]{:S(2)}) async-start(), calls=%async_computation.9 | async-start | bytes 1327104 | tf_op jit(solution)/shard_map/all_gather | solution.py:91
  10.1 105.2 %all-gather.11.cloned.1.call-start = ((), (), s32[]{:S(2)}) async-start(), calls=%async_computation.10 | async-start | bytes 5308416 | tf_op jit(solution)/shard_map/all_gather | solution.py:92
  12.3 169.1 %all-gather.15.cloned.1.call-start = ((), (), s32[]{:S(2)}) async-start(), calls=%async_computation.12 | async-start | bytes 11943936 | tf_op jit(solution)/shard_map/all_gather | solution.py:94
  13.7 209.0 %all-gather.13.cloned.1.call-start = ((), (), s32[]{:S(2)}) async-start(), calls=%async_computation.11 | async-start | bytes 5308416 | tf_op jit(solution)/shard_map/all_gather | solution.py:93
  13.8 18.8 %collective-permute-start.2 = (bf16[1,1,32,768]{3,2,1,0:T(8,128)(2,1)S(1)}, bf16[1,1,32,768]{3,2,1,0:T(8,128)(2,1)S(1)}, u32[]{:S(2)}, u32[]{:S(2)}) collective-permute-start(bf16[1,1,32,768]{3,2,1,0:T(8,128)(2,1)S(1)} %get-tuple-element.82), channel_id=1, source_target_pairs={{0,8},{8,16},{16,24},{1,9},{9,17},{17,25},{2,10},{10,18},{18,26},{... | collective-permute-start | bytes 147464 | tf_op jit(solution)/shard_map/ppermute | solution.py:25
  18.8 13.8 %collective-permute-start.3 = (bf16[1,1,32,768]{3,2,1,0:T(8,128)(2,1)S(1)}, bf16[1,1,32,768]{3,2,1,0:T(8,128)(2,1)S(1)}, u32[]{:S(2)}, u32[]{:S(2)}) collective-permute-start(bf16[1,1,32,768]{3,2,1,0:T(8,128)(2,1)S(1)} %get-tuple-element.83), channel_id=1, source_target_pairs={{8,0},{16,8},{24,16},{9,1},{17,9},{25,17},{10,2},{18,10},{26,18},{... | collective-permute-start | bytes 147464 | tf_op jit(solution)/shard_map/ppermute | solution.py:27
  21.0 257.7 %reduce-scatter.13.cloned.1.call-start = ((), (), s32[]{:S(2)}) async-start(), calls=%async_computation.14 | async-start | bytes 1966080 | tf_op jit(solution)/shard_map/reduce_scatter | solution.py:218
  22.0 27.9 %copy-start.66 = (f32[128]{0:T(128)}, f32[128]{0:T(128)S(1)}, u32[]{:S(2)}) copy-start(f32[128]{0:T(128)S(1)} %div.108) | copy-start | bytes 1540
  31.0 18.9 %copy-start.55 = (f32[768]{0:T(1024)}, f32[768]{0:T(1024)S(1)}, u32[]{:S(2)}) copy-start(f32[768]{0:T(1024)S(1)} %get-tuple-element.41) | copy-start | bytes 9220
  31.7 18.2 %copy-start.73 = (f32[128]{0:T(128)}, f32[128]{0:T(128)S(1)}, u32[]{:S(2)}) copy-start(f32[128]{0:T(128)S(1)} %fusion.65) | copy-start | bytes 1540
  243.3 72.0 %reduce-scatter.11.cloned.1.call-start = ((), (), s32[]{:S(2)}) async-start(), calls=%async_computation.13 | async-start | bytes 1966080 | tf_op jit(solution)/shard_map/reduce_scatter | solution.py:215
  248.4 122.5 %reduce-scatter.17.cloned.1.call-start = ((), (), s32[]{:S(2)}) async-start(), calls=%async_computation.16 | async-start | bytes 2654208 | tf_op jit(solution)/shard_map/reduce_scatter | solution.py:237
  251.3 65.0 %copy-start.31 = (bf16[128,768]{1,0:T(8,128)(2,1)S(1)}, bf16[128,768]{1,0:T(8,128)(2,1)}, u32[]{:S(2)}) copy-start(bf16[128,768]{1,0:T(8,128)(2,1)} %copy-done.30) | copy-start | bytes 589828
  251.4 178.8 %reduce-scatter.15.cloned.1.call-start = ((), (), s32[]{:S(2)}) async-start(), calls=%async_computation.15 | async-start | bytes 7962624 | tf_op jit(solution)/shard_map/reduce_scatter | solution.py:236
  279.7 40.6 %copy-start.43 = (bf16[128,768]{0,1:T(8,128)(2,1)}, bf16[128,768]{0,1:T(8,128)(2,1)S(1)}, u32[]{:S(2)}) copy-start(bf16[128,768]{0,1:T(8,128)(2,1)S(1)} %convert_bitcast_fusion) | copy-start | bytes 589828
  320.3 189.7 %reduce-scatter.19.cloned.1.call-start = ((), (), s32[]{:S(2)}) async-start(), calls=%async_computation.17 | async-start | bytes 10616832 | tf_op jit(solution)/shard_map/reduce_scatter | solution.py:238
  326.6 263.5 %reduce-scatter.21.cloned.1.call-start = ((), (), s32[]{:S(2)}) async-start(), calls=%async_computation.18 | async-start | bytes 10616832 | tf_op jit(solution)/shard_map/reduce_scatter | solution.py:239
  334.9 395.9 %reduce-scatter.23.cloned.1.call-start = ((), (), s32[]{:S(2)}) async-start(), calls=%async_computation.19 | async-start | bytes 23887872 | tf_op jit(solution)/shard_map/reduce_scatter | solution.py:240
  339.0 4.0 collective-permute-start
  341.2 6.0 collective-permute-start.1
  364.8 403.5 %reduce-scatter.25.cloned.1.call-start = ((), (), s32[]{:S(2)}) async-start(), calls=%async_computation.20 | async-start | bytes 442368
  370.6 621.3 %all-reduce.5.cloned.1.call-start = ((), (), s32[]{:S(2)}) async-start(), calls=%async_computation.21 | async-start | bytes 12386304 | tf_op jit(solution)/shard_map/psum | solution.py:243
  743.6 37.3 %copy-start.69 = (f32[4,96]{1,0:T(4,128)S(1)}, f32[4,96]{1,0:T(4,128)}, u32[]{:S(2)}) copy-start(f32[4,96]{1,0:T(4,128)} %param.41) | copy-start | bytes 4612
  743.7 37.3 %copy-start.75 = (f32[4,96]{1,0:T(4,128)S(1)}, f32[4,96]{1,0:T(4,128)}, u32[]{:S(2)}) copy-start(f32[4,96]{1,0:T(4,128)} %param.43) | copy-start | bytes 4612
  743.7 37.3 %copy-start.76 = (f32[4,96]{1,0:T(4,128)S(1)}, f32[4,96]{1,0:T(4,128)}, u32[]{:S(2)}) copy-start(f32[4,96]{1,0:T(4,128)} %param.42) | copy-start | bytes 4612
  743.7 248.2 %copy-start.38 = (f32[96,768]{1,0:T(8,128)S(1)}, f32[96,768]{1,0:T(8,128)}, u32[]{:S(2)}) copy-start(f32[96,768]{1,0:T(8,128)} %param.29) | copy-start | bytes 884740
  743.7 248.2 %copy-start.47 = (f32[96,768]{1,0:T(8,128)S(1)}, f32[96,768]{1,0:T(8,128)}, u32[]{:S(2)}) copy-start(f32[96,768]{1,0:T(8,128)} %param.31) | copy-start | bytes 884740
  746.1 245.8 %copy-start.48 = (f32[96,768]{1,0:T(8,128)S(1)}, f32[96,768]{1,0:T(8,128)}, u32[]{:S(2)}) copy-start(f32[96,768]{1,0:T(8,128)} %param.30) | copy-start | bytes 884740
  746.1 247.9 %copy-start.22 = (f32[96,2304]{1,0:T(8,128)S(1)}, f32[96,2304]{1,0:T(8,128)}, u32[]{:S(2)}) copy-start(f32[96,2304]{1,0:T(8,128)} %param.26) | copy-start | bytes 2654212
  747.0 247.0 %copy-start.40 = (f32[96,2304]{1,0:T(8,128)S(1)}, f32[96,2304]{1,0:T(8,128)}, u32[]{:S(2)}) copy-start(f32[96,2304]{1,0:T(8,128)} %param.28) | copy-start | bytes 2654212
  781.0 216.6 %copy-start.70 = (f32[4,96]{1,0:T(4,128)}, f32[4,96]{1,0:T(4,128)S(1)}, u32[]{:S(2)}) copy-start(f32[4,96]{1,0:T(4,128)S(1)} %psum.47) | copy-start | bytes 4612
  (69 other events, 271.4 us)
Sparse Core Ops, SparseCore 0:
  10.5 36.6 all-gather.6
  49.7 24.0 all-gather.8
  76.2 38.9 all-gather.10
  117.6 63.8 all-gather.14
  183.7 38.9 all-gather.12
  243.4 35.2 reduce-scatter.12
  281.0 34.2 reduce-scatter.10
  319.2 41.4 reduce-scatter.16
  364.6 65.5 reduce-scatter.14
  433.5 76.4 reduce-scatter.18
  513.5 76.4 reduce-scatter.20
  593.5 137.1 reduce-scatter.22
  734.4 33.8 reduce-scatter.24
  770.9 220.9 all-reduce.4
where the time goes:
time: 1030 us; the launch traced here: 1020 us
  waiting for transfers between devices  772 us (75%)
  matrix products  107 us (10%)
  blocking collectives  58.3 us (6%)
  other arithmetic  33.9 us (3%)
  local copies, waits for them, and re-layouts  26.6 us (3%)
  between operations  16 us (2%)
  starting transfers between devices  10.7 us (1%)
    psum x1, waiting for transfers between devices, per_device(): lax.psum((partial_shares[0], partial_shares[1], partial_shares[2], partia...  210 us
    reduce_scatter x1, waiting for transfers between devices, per_device(): lax.psum_scatter(kernel_grad, 'col', scatter_dimension=1, tiled=True)  141 us
    reduce_scatter x1, waiting for transfers between devices, per_device(): lax.psum_scatter(shrink_grad, 'col', scatter_dimension=0, tiled=True)  80 us
    reduce_scatter x1, waiting for transfers between devices, per_device(): lax.psum_scatter(expand_grad, 'col', scatter_dimension=0, tiled=True)  79.9 us
    all_gather x1, waiting for transfers between devices, per_device(): lax.all_gather(kernel_weight.astype(jnp.bfloat16), 'col', axis=1, tiled=T...  61.8 us
    reduce_scatter x1, waiting for transfers between devices, per_device(): lax.psum_scatter(heads_grad, 'col', scatter_dimension=0, tiled=True)  59.3 us
    reduce_scatter x1, waiting for transfers between devices, per_device(): lax.psum_scatter(key_terms.reshape(images, -1, model_width), 'row', scatt...  35.6 us
    reduce_scatter x1, waiting for transfers between devices, per_device(): lax.psum_scatter(value_terms.reshape(images, -1, model_width), 'row', sca...  25.2 us
  transfers between devices with their start and end apart: 18, of which 14 were waited for; matrix products, arithmetic and copies ran while one was open for 11% of the time, Pallas kernels for 0%

commit v1 on v0

v1 whole, which is shorter than its diff:
```python
import functools
import types

import jax
import jax.numpy as jnp
from jax import lax
from jax.experimental import pallas as pl
from jax.experimental.pallas import tpu as pltpu
from jax.sharding import PartitionSpec as P

D = 768
HEADS = 12
HEAD_DIM = 64
FF = 3072
STEP = 5
TEAM = 8

beta_first = 0.5
beta_second = 0.5

MESH = pl.DeviceIdType.MESH
F32 = jnp.float32
BF16 = jnp.bfloat16


def layer_norm(values, norm_gain, norm_shift):
    center = values - jnp.mean(values, axis=-1, keepdims=True)
    spread = jnp.mean(center * center, axis=-1, keepdims=True)
    return center * lax.rsqrt(spread + 1e-05) * norm_gain + norm_shift


def exact_gelu(values):
    return jax.nn.gelu(values, approximate=False)


def step_rates():
    return (D ** (-0.5), 8.0 * D ** (-0.5), D ** (-0.5), FF ** (-0.5), (9 * D) ** (-0.5), 0.3)


def adam_body(plan, counts, *refs):
    params, passed = counts
    taken = 4 * params + 4 + passed
    given, results = refs[:taken], refs[taken : taken + 5 * params + 5 + passed]
    scratch = refs[taken + len(results) :]
    in_sem, out_sem = scratch[-2:]
    norm_in, norm_out = given[4 * params : 4 * params + 4], results[5 * params : 5 * params + 5]
    through = [
        pltpu.make_async_copy(src, dst, out_sem.at[len(plan), at])
        for at, (src, dst) in enumerate(zip(given[4 * params + 4 :], results[5 * params + 5 :]))
    ]

    def cut(ref, taps):
        return ref if taps is None else ref.at[pl.ds(*taps)]

    loads = []
    for at, (param, taps) in enumerate(plan):
        grads, values, _ = scratch[3 * at : 3 * at + 3]
        into = [grads] + [values.at[index] for index in range(3)]
        made = [
            pltpu.make_async_copy(cut(ref, taps), dst, in_sem.at[at, index])
            for index, (ref, dst) in enumerate(zip(given[4 * param : 4 * param + 4], into))
        ]
        for each in made:
            each.start()
        loads.append(made)
    for each in through:
        each.start()
    rates = step_rates()
    gradient = norm_in[0][pl.ds(0, 4), pl.ds(0, norm_in[1].shape[1])]
    updated = adam_update(norm_in[1][...], norm_in[2][...], norm_in[3][...], gradient, rates[5])
    for ref, value in zip(norm_out, updated):
        ref[...] = value
    stores = []
    for at, (param, taps) in enumerate(plan):
        grads, values, copies = scratch[3 * at : 3 * at + 3]
        for each in loads[at]:
            each.wait()
        rows, columns = grads.shape[-2:]
        deep = 16 if rows % 16 == 0 else rows
        wide = D if columns % D == 0 else columns
        leads = range(grads.shape[0]) if grads.ndim == 3 else (None,)

        def update(step, carry):
            inside = pl.ds(pl.multiple_of(step * deep, deep), deep) if deep < rows else slice(None)
            for lead in leads:
                for begin in range(0, columns, wide):
                    spot = (inside, pl.ds(begin, wide))
                    spot = spot if lead is None else (lead,) + spot
                    updated = adam_update(
                        *(values[(index,) + spot] for index in range(3)),
                        grads[spot].astype(F32),
                        rates[param],
                    )
                    for index, value in zip((3, 1, 2, 0), updated):
                        values[(index,) + spot] = value
                    copies[spot] = updated[4]
            return carry

        if deep < rows:
            lax.fori_loop(0, rows // deep, update, 0)
        else:
            update(0, 0)
        sources = [values.at[index] for index in (3, 1, 2, 0)] + [copies]
        for index, src in enumerate(sources):
            dst = cut(results[5 * param + index], taps)
            made = pltpu.make_async_copy(src, dst, out_sem.at[at, index])
            made.start()
            stores.append(made)
    for each in stores + through:
        each.wait()


def adam_all(params, norm, passed):
    plan = []
    for at, (_, master, _, _) in enumerate(params):
        if master.ndim == 3:
            plan += [(at, (tap, 3)) for tap in range(0, master.shape[0], 3)]
        else:
            plan.append((at, None))
    plan.sort(key=lambda block: -params[block[0]][1].size)
    any_at, vmem = pl.BlockSpec(memory_space=pl.ANY), pl.BlockSpec(memory_space=pltpu.VMEM)
    results = [
        jax.ShapeDtypeStruct(group[1].shape, dtype)
        for group in [*params, norm]
        for dtype in (F32, F32, F32, F32, BF16)
    ] + [jax.ShapeDtypeStruct(array.shape, array.dtype) for array in passed]
    scratch = []
    for at, taps in plan:
        grads, master = params[at][:2]
        shape = master.shape if taps is None else (taps[1],) + master.shape[1:]
        scratch += [
            pltpu.VMEM(shape, grads.dtype),
            pltpu.VMEM((4,) + shape, F32),
            pltpu.VMEM(shape, BF16),
        ]
    flat = [array for group in params for array in group]
    return pl.pallas_call(
        functools.partial(adam_body, plan, (len(params), len(passed))),
        out_shape=results,
        in_specs=[any_at] * len(flat) + [vmem] * 4 + [any_at] * len(passed),
        out_specs=[any_at] * (5 * len(params)) + [vmem] * 5 + [any_at] * len(passed),
        scratch_shapes=scratch
        + [
            pltpu.SemaphoreType.DMA((len(plan), 4)),
            pltpu.SemaphoreType.DMA((len(plan) + 1, 5)),
        ],
        compiler_params=pltpu.CompilerParams(vmem_limit_bytes=60 << 20),
        cost_estimate=pl.CostEstimate(
            flops=20 * sum(group[1].size for group in params),
            bytes_accessed=30 * sum(group[1].size for group in params),
            transcendentals=0,
        ),
        name="adam",
    )(*flat, *norm, *passed)


def adam_update(master, moment_one, moment_two, gradient, step_rate):
    new_mean = beta_first * (moment_one + gradient)
    new_square = beta_second * (moment_two + gradient * gradient)
    square_hat = new_square * (1.0 / (1.0 - beta_second**STEP))
    root = square_hat * lax.rsqrt(square_hat) + 1e-08
    inverse = pl.reciprocal(root, approx=True)
    inverse = inverse * (2.0 - root * inverse)
    toward = new_mean * inverse
    new_master = master * (1.0 - 0.01 * step_rate) - toward * (
        step_rate / (1.0 - beta_first**STEP)
    )
    return (gradient, new_mean, new_square, new_master, new_master.astype(jnp.bfloat16))


def dot(a, b, dims):
    return lax.dot_general(a, b, (dims, ((), ())), preferred_element_type=F32)


def place():
    teams = lax.axis_size("col") // TEAM
    row, col = lax.axis_index("row"), lax.axis_index("col")
    at, team = col // teams, col % teams

    def device(row_at, chip_at, core_at):
        return (row_at, (chip_at * 2 + core_at) * teams + team)

    return row, at // 2, at % 2, device


def dot_in(a, b):
    return dot(a, b, ((1,), (0,)))


def dot_right(a, b):
    return dot(a, b, ((1,), (1,)))


def dot_left(a, b):
    return dot(a, b, ((0,), (0,)))


def greet(devices):
    barrier = pltpu.get_barrier_semaphore()
    for device in devices:
        pl.semaphore_signal(barrier, inc=1, device_id=device, device_id_type=MESH)
    return lambda: pl.semaphore_wait(barrier, len(devices))


KINDS = (
    "patches",
    "heads",
    "norm",
    "grads",
    "usable",
    "merge",
    "expand",
    "attended",
    "rim_up",
    "rim_down",
    "normed_two",
    "down",
    "feed",
    "normed_two_grad",
    "expand_back",
    "cells",
    "above",
    "below",
    "attended_grad",
    "merge_back",
    "normed_in",
    "normed_over",
    "normed_out",
    "pixels",
    "heads_back",
    "heads_rows",
    "norm_back",
    "norm_rows",
)
PAIRS = (
    "grads",
    "cells",
    "heads",
    "merge",
    "expand",
    "kernel",
    "shrink",
    "shrink_back",
    "expand_back",
    "merge_back",
    "heads_back",
)


def layer_body(sizes, names, *refs):
    rows, half, share, grid_cols, heads_here = sizes
    v = types.SimpleNamespace(**dict(zip(names, refs)))
    row, quad, core, device_at = place()
    sibling = device_at(row, quad, 1 - core)
    team = 2 * half
    at = quad * 2 + core
    local, width = v.patches.shape
    length = rows * local
    block = width // half
    head_part = width // rows
    own_rows = half * share
    is_end = jnp.logical_or(row == 0, row == rows - 1)
    is_middle = jnp.logical_not(is_end)
    toward = jnp.where(row < rows // 2, 1, -1)
    inner = device_at(lax.rem(row + toward + rows, rows), quad, core)
    outer = device_at(lax.rem(row - toward + rows, rows), quad, core)

    def turn(base, step, count):
        return lax.rem(base + count + step, count)

    def across(step):
        return (quad, quad + 1 - 2 * (quad % 2), quad + 2 - 4 * (quad // 2), 3 - quad)[step]

    def on_chip(step, shift=0):
        return device_at(turn(row, shift, rows), across(step), core)

    def on_row(step):
        return device_at(turn(row, step, rows), quad, core)

    def on_team(step):
        there = turn(at, step, team)
        return device_at(row, there // 2, lax.rem(there, 2))

    all_here = greet(
        [on_team(step) for step in range(1, team)]
        + [on_row(step) for step in range(1, rows)]
        + [on_chip(step, shift) for shift in (-1, 1) for step in range(half)]
    )

    started = []

    def link(kind, index, src, dst, device):
        return pltpu.make_async_remote_copy(
            src_ref=src,
            dst_ref=dst,
            send_sem=v.send_sem.at[KINDS.index(kind), index],
            recv_sem=v.recv_sem.at[KINDS.index(kind), index],
            device_id=device,
            device_id_type=MESH,
        )

    def pair(kind, index, src, dst):
        return pltpu.make_async_remote_copy(
            src_ref=src,
            dst_ref=dst,
            send_sem=v.pair_send.at[PAIRS.index(kind), index],
            recv_sem=v.pair_recv.at[PAIRS.index(kind), index],
            device_id=sibling,
            device_id_type=MESH,
        )

    def start(made):
        made.start()
        started.append(made)
        return made

    def arrived(made):
        for each in made:
            each.wait_recv()

    def gone(made):
        for each in made:
            each.wait_send()
            started[:] = [other for other in started if other is not each]

    def to_chips(kind, src, dst):
        return [
            start(link(kind, step, src(across(step)), dst(step), on_chip(step)))
            for step in range(1, half)
        ]

    def to_rows(kind, src, dst):
        return [
            start(link(kind, step, src(turn(row, step, rows)), dst, on_row(step)))
            for step in range(1, rows)
        ]

    def share_of(ref, chip, core_at):
        return ref.at[pl.ds(pl.multiple_of((chip * 2 + core_at) * share, share), share)]

    def line(kind, j, src, dst, device):
        return pltpu.make_async_remote_copy(
            src_ref=src,
            dst_ref=dst,
            send_sem=v.line_send.at[kind, j],
            recv_sem=v.line_recv.at[kind, j],
            device_id=device,
            device_id_type=MESH,
        )

    chunks = v.line_got.shape[0]

    def line_inward(j):
        return line(0, j, v.line_got.at[j], v.line_got.at[j], inner)

    def line_over(j):
        return line(1, j, v.line_got.at[j], line_result(j), inner)

    def line_result(j):
        if j < half:
            return v.shrink_here.at[pl.ds(j * share, share)]
        if j < 2 * half:
            return v.expand_sum.at[j - half]
        if j < chunks - 1:
            return v.kernel_here.at[j - 2 * half]
        return v.merge_here

    def line_outward(j):
        return line(2, j, line_result(j), line_result(j), outer)

    ready, done_in, done_over = [], [0], [0]

    def line_ready(j, value):
        @pl.when(is_end)
        def _():
            v.line_got[j] = value().astype(BF16)
            line_inward(j).start()

        ready.append((j, value))

    def line_step(count=1):
        for _ in range(count):
            if done_in[0] < len(ready):
                j, value = ready[done_in[0]]
                done_in[0] += 1

                @pl.when(is_middle)
                def _():
                    line_inward(j).wait_recv()
                    v.line_got[j] = (value() + v.line_got[j].astype(F32)).astype(BF16)
                    line_over(j).start()

            behind = 2 if done_in[0] < chunks else 0
            if done_over[0] + behind <= done_in[0] and done_over[0] < done_in[0]:
                k = ready[done_over[0]][0]
                done_over[0] += 1

                @pl.when(is_middle)
                def _():
                    line_over(k).wait_recv()
                    total = v.line_got[k].astype(F32) + line_result(k)[...].astype(F32)
                    line_result(k)[...] = total.astype(BF16)
                    line_outward(k).start()

    def fetch(index, src, dst):
        made = pltpu.make_async_copy(src, dst, v.own_sem.at[index])
        made.start()
        return made

    heads_in = [
        fetch(
            3 + half + part,
            v.heads.at[:, pl.ds(part * width, width)],
            v.slope.at[part, pl.ds(0, share)],
        )
        for part in range(3)
    ]
    kernel_in = fetch(0, v.kernel, v.kernel_kept)
    merge_in = fetch(1, v.merge, v.slope.at[half - 1, pl.ds(0, share)])
    expand_in = [
        fetch(2 + chip, v.expand.at[:, pl.ds(chip * width, width)], v.expand_kept.at[chip])
        for chip in range(half)
    ]
    shrink_in = fetch(2 + half, v.shrink, v.grad.at[pl.ds(0, own_rows)])
    v.patches_all[row] = v.patches[...]
    v.grads_all[0] = v.grads[...]
    extent = v.widths[0]
    column = lax.broadcasted_iota(jnp.int32, (1, grid_cols), 1)
    corner = lax.broadcasted_iota(jnp.int32, (grid_cols, grid_cols), 0)
    corner = corner == lax.broadcasted_iota(jnp.int32, (grid_cols, grid_cols), 1)

    def usable_row(y):
        held = jnp.logical_and(v.patch_mask[pl.ds(y, 1), :] == 1, column < extent)
        return jnp.where(held, 1.0, 0.0)

    grid_rows = local // grid_cols
    for y in range(rows * grid_rows):
        v.key_valid[:, pl.ds(y * grid_cols, grid_cols)] = usable_row(y)
    for y in range(grid_rows):
        turned = jnp.where(corner, usable_row(row * grid_rows + y), 0.0)
        turned = jnp.sum(turned, axis=1, keepdims=True)
        v.usable[pl.ds(y * grid_cols, grid_cols), :] = jnp.broadcast_to(
            turned, (grid_cols, 128)
        ).astype(BF16)
    v.usable_all[0] = v.usable[...]
    v.norm_low[...] = jnp.zeros_like(v.norm_low)
    v.norm_low[pl.ds(0, 4), pl.ds(0, share)] = v.norm_table[...].astype(BF16).astype(F32)
    v.norm_got[at] = v.norm_low[...]
    for each in heads_in:
        each.wait()
    for there in range(rows):

        @pl.when(row == there)
        def _():
            for part in range(3):
                taken = v.slope[part, pl.ds(0, share), pl.ds(there * head_part, head_part)]
                v.heads_low[:, pl.ds(part * head_part, head_part)] = taken.astype(BF16)

    taps = 9 * share
    wide_taps = v.kernel_all.shape[1]
    kernel_in.wait()
    for tap in range(9):
        v.kernel_all[core, pl.ds(tap * share, share), :] = v.kernel_kept[tap].astype(BF16)
    padding = jnp.zeros((wide_taps - taps, width), BF16)
    for side in range(2):
        v.kernel_all[side, pl.ds(taps, wide_taps - taps), :] = padding

    all_here()
    patches_sent = to_rows("patches", lambda there: v.patches, v.patches_all.at[row])
    mine = v.kernel_all.at[core, pl.ds(0, taps)]
    kernel_sent = start(pair("kernel", 0, mine, mine))
    grads_sent = to_chips("grads", lambda there: v.grads, v.grads_all.at.__getitem__)

    def spread(kind, src, ref):
        mine = share_of(ref, quad, core)
        sent = to_chips(kind, src, lambda step: mine)
        mine[...] = src(quad)[...]
        forward = [start(pair(kind, 0, mine, mine))]
        return sent, forward

    def forwarded(kind, ref, spreading):
        sent, forward = spreading
        for step in range(1, half):
            sent[step - 1].wait_recv()
            there = share_of(ref, across(step), core)
            forward.append(start(pair(kind, step, there, there)))
        return forward

    heads_sent = spread("heads", lambda there: v.heads_low, v.heads_all)
    norm_sent = [
        start(link("norm", step, v.norm_low, v.norm_got.at[at], on_team(step)))
        for step in range(1, team)
    ]
    usable_sent = to_chips("usable", lambda there: v.usable, v.usable_all.at.__getitem__)
    merge_in.wait()
    v.merge_low[...] = v.slope[half - 1, pl.ds(0, share)].astype(BF16)
    merge_sent = spread("merge", lambda there: v.merge_low, v.merge_all)
    for chip in range(half):
        expand_in[chip].wait()
        v.expand_send[chip] = v.expand_kept[chip].astype(BF16)
    expand_sent = spread("expand", lambda there: v.expand_send.at[there], v.expand_all)
    shrink_mine = pl.ds(pl.multiple_of(core * own_rows, own_rows), own_rows)
    shrink_in.wait()
    v.shrink_all[shrink_mine, :] = v.grad[pl.ds(0, own_rows), :].astype(BF16)
    mine = v.shrink_all.at[shrink_mine]
    shrink_sent = start(pair("shrink", 0, mine, mine))

    tall = local + 2 * grid_cols
    spot = lax.rem(lax.broadcasted_iota(jnp.int32, (tall, block), 0), grid_cols)
    not_first, not_last = spot != 0, spot != grid_cols - 1

    def rim(b, slot, begin, size, lane=0, lanes=block):
        rows_at, lanes_at = slot // 2 * tall + begin, slot % 2 * (length // 2) + lane
        return b, pl.ds(rows_at, size), pl.ds(lanes_at, lanes)

    def pixels_back(first, last):
        count = last - first
        here = v.grads_all[pl.ds(first, count)].reshape(count * local, width)
        empty = jnp.zeros((2 * grid_cols, block), F32)
        for slot in range(count):
            for b in range(3):
                v.probs[rim(b, slot, local, 2 * grid_cols)] = empty
        for side in range(2):
            every = dot_right(here, v.kernel_all[side])
            for tap in range(9):
                a, b = tap // 3, tap % 3
                term = every[:, tap * share : (tap + 1) * share].reshape(count, local, share)
                for slot in range(count):
                    into = rim(b, slot, a * grid_cols, local, side * share, share)
                    if a == 0:
                        v.probs[into] = term[slot]
                    else:
                        v.probs[into] += term[slot]
        for slot in range(first, last):
            ahead, center, back = (v.probs[rim(b, slot - first, 0, tall)] for b in range(3))
            ahead = jnp.where(not_first, ahead, 0.0)
            back = jnp.where(not_last, back, 0.0)
            whole = (
                center
                + jnp.concatenate([ahead[1:], ahead[:1]], axis=0)
                + jnp.concatenate([back[tall - 1 :], back[: tall - 1]], axis=0)
            )
            v.rim_up_send[slot] = whole[:grid_cols].astype(BF16)
            v.rim_down_send[slot] = whole[tall - grid_cols :].astype(BF16)
            v.feed_part[slot] = whole[grid_cols : tall - grid_cols]

    kernel_sent.wait_recv()
    pixels_back(0, 1)
    arrived(grads_sent)
    grads_pair = start(pair("grads", 0, v.grads_all, v.grads_other))
    pixels_back(1, half)
    rims = [
        start(link("rim_up", 0, v.rim_up_send, v.rim_below, on_row(-1))),
        start(link("rim_down", 0, v.rim_down_send, v.rim_above, on_row(1))),
    ]

    heads_done = forwarded("heads", v.heads_all, heads_sent)
    arrived(norm_sent)
    for there in range(team):
        v.gains[:, pl.ds(there * share, share)] = v.norm_got[there, :, pl.ds(0, share)]

    def normal(values):
        center = values - jnp.mean(values, axis=-1, keepdims=True)
        spread_here = jnp.mean(center * center, axis=-1, keepdims=True)
        scale = lax.rsqrt(spread_here + 1e-05)
        return center * scale, scale

    arrived(patches_sent)
    for there in range(rows):
        hat, _ = normal(v.patches_all[there].astype(F32))
        normed = (hat * v.gains[0:1] + v.gains[1:2]).astype(BF16)
        v.normed[pl.ds(there * local, local), :] = normed
    arrived(heads_done)
    v.projected[...] = dot_in(v.normed[...], v.heads_all[...]).astype(BF16)

    def part_of(ref, part, head):
        return ref[:, pl.ds(part * head_part + head * HEAD_DIM, HEAD_DIM)]

    def attend(there):
        inside = pl.ds(pl.multiple_of(there * local, local), local)
        for head in range(heads_here):
            queries = v.projected[inside, pl.ds(head * HEAD_DIM, HEAD_DIM)]
            queries = queries * jnp.asarray(0.125, BF16)
            scores = dot_right(queries, part_of(v.projected, 1, head))
            scores = jnp.where(v.key_valid[...] > 0.0, scores, -1e30)
            risen = jnp.exp(scores - jnp.max(scores, axis=-1, keepdims=True))
            probs = risen * (1.0 / jnp.sum(risen, axis=-1, keepdims=True))
            v.probs[head, inside, :] = probs
            taken = dot_in(probs.astype(BF16), part_of(v.projected, 2, head))
            v.attended_send[there, :, pl.ds(head * HEAD_DIM, HEAD_DIM)] = taken.astype(BF16)

    attended_sent = []
    for step in range(1, rows):
        there = turn(row, step, rows)
        attend(there)
        src, dst = v.attended_send.at[there], v.attended_got.at[row]
        attended_sent.append(start(link("attended", step, src, dst, on_row(step))))
        if step == 2:
            arrived(usable_sent)
            arrived(rims)
            for slot in range(half):
                first, last = pl.ds(0, grid_cols), pl.ds(local - grid_cols, grid_cols)
                above = jnp.where(row > 0, v.rim_above[slot].astype(F32), 0.0)
                below = jnp.where(row < rows - 1, v.rim_below[slot].astype(F32), 0.0)
                v.feed_part[slot, first, :] += above
                v.feed_part[slot, last, :] += below
                kept = v.usable_all[slot, :, pl.ds(0, 1)].astype(F32) > 0.0
                v.down_got[quad, slot] = jnp.where(kept, v.feed_part[slot], 0.0).astype(BF16)
            down_sent = to_chips(
                "down", lambda there: v.down_got.at[quad], lambda step: v.down_got.at[quad]
            )
    attend(row)
    v.attended_got[row] = v.attended_send[row]
    merge_done = forwarded("merge", v.merge_all, merge_sent)
    expand_done = forwarded("expand", v.expand_all, expand_sent)

    v.normed_turned[...] = v.normed[...].T
    arrived(attended_sent)
    for there in range(rows):
        v.attended[:, pl.ds(there * head_part, head_part)] = v.attended_got[there]
    arrived(merge_done)
    after_attend = v.patches[...].astype(F32) + dot_in(v.attended[...], v.merge_all[...])
    v.after_attend[...] = after_attend
    hat, _ = normal(after_attend)
    v.normed_two[0] = (hat * v.gains[2:3] + v.gains[3:4]).astype(BF16)
    normed_two_sent = to_chips(
        "normed_two", lambda there: v.normed_two.at[0], v.normed_two.at.__getitem__
    )

    arrived(expand_done)
    shrink_sent.wait_recv()

    def stack(ref, first, last):
        return ref[pl.ds(first, last - first)].reshape((last - first) * local, ref.shape[-1])

    def place_in(ref, first, last, value):
        ref[pl.ds(first, last - first)] = value.reshape(last - first, local, ref.shape[-1])

    def forward(first, last):
        hidden = dot_in(stack(v.normed_two, first, last), v.expand_all[...])
        below = 0.5 * (1.0 + lax.erf(hidden * (0.5**0.5)))
        density = jnp.exp(-0.5 * hidden * hidden) * ((2.0 * 3.141592653589793) ** -0.5)
        place_in(v.slope, first, last, below + hidden * density)
        place_in(v.active, first, last, (hidden * below).astype(BF16))
        whole = dot_in(stack(v.active, first, last), v.shrink_all[...])
        place_in(v.feed_send, first, last, whole.astype(BF16))

    def backward(first, last):
        grad_here = dot_right(stack(v.down_in, first, last), v.shrink_all[...])
        grad_here = (grad_here * stack(v.slope, first, last)).astype(BF16)
        place_in(v.hidden_grad, first, last, grad_here)
        whole = dot_right(stack(v.hidden_grad, first, last), v.expand_all[...])
        place_in(v.normed_two_send, first, last, whole.astype(BF16))

    def send_back(kind, send, got, steps=(1, 2, 3)):
        if 1 in steps:
            got[0] = send[0]
        return [
            start(link(kind, step, send.at[step], got.at[step], on_chip(step)))
            for step in steps
        ]

    def flat(ref):
        return stack(ref, 0, half)

    v.attended_turned[...] = v.attended[...].T
    forward(0, 1)
    arrived(down_sent)
    for slot in range(half):
        for chip in range(half):
            v.down_in[slot, :, pl.ds(chip * block, block)] = v.down_got[chip, across(chip ^ slot)]
    backward(0, 1)
    arrived(normed_two_sent[:2])
    forward(1, half - 1)
    feed_sent = send_back("feed", v.feed_send, v.feed_got, (1, 2))
    arrived(normed_two_sent[2:])
    forward(half - 1, half)
    feed_sent += send_back("feed", v.feed_send, v.feed_got, (3,))
    v.grad[...] = dot_left(flat(v.active), flat(v.down_in))
    at_other = pl.multiple_of((1 - core) * own_rows, own_rows)
    v.shrink_send[...] = v.grad[pl.ds(at_other, own_rows), :].astype(BF16)
    shrink_back = start(pair("shrink_back", 0, v.shrink_send, v.shrink_got))
    backward(1, half)
    shrink_back.wait_recv()
    for j in range(half):

        def shrink_chunk(j=j):
            begin = pl.multiple_of(core * own_rows + j * share, share)
            inside = pl.ds(j * share, share)
            return v.grad[pl.ds(begin, share), :] + v.shrink_got[inside, :].astype(F32)

        line_ready(j, shrink_chunk)

    def split(value, kept, sent, lanes=slice(None)):
        for chip in range(half):
            begin = 2 * chip * share
            first, second = value[begin : begin + share], value[begin + share : begin + 2 * share]
            kept[chip, :, lanes] = jnp.where(core == 0, first, second)
            sent[chip] = jnp.where(core == 0, second, first).astype(BF16)

    arrived(feed_sent)
    after_feed = v.after_attend[...] + jnp.sum(v.feed_got[...].astype(F32), axis=0)
    kept = v.usable[:, pl.ds(0, 1)].astype(F32) > 0.0
    cells_here = jnp.where(kept, after_feed, 0.0).astype(BF16)
    for chip in range(half):
        v.cells_send[chip] = cells_here[:, chip * block : (chip + 1) * block]
    v.cells_got[0] = v.cells_send[quad]
    cells_sent = to_chips(
        "cells", lambda there: v.cells_send.at[there], v.cells_got.at.__getitem__
    )
    for step in range(half):
        there = across(step)
        head = v.cells_send.at[there, pl.ds(0, grid_cols)]
        foot = v.cells_send.at[there, pl.ds(local - grid_cols, grid_cols)]
        dst = v.below_got.at[step]
        cells_sent.append(start(link("below", step, head, dst, on_chip(step, -1))))
        dst = v.above_got.at[step]
        cells_sent.append(start(link("above", step, foot, dst, on_chip(step, 1))))
    normed_two_back = send_back("normed_two_grad", v.normed_two_send, v.normed_two_got)
    gone(expand_sent[0])
    split(dot_left(flat(v.normed_two), flat(v.hidden_grad)), v.expand_kept, v.expand_send)
    expand_pair = start(pair("expand_back", 0, v.expand_send, v.expand_got))

    line_step()

    expand_pair.wait_recv()
    for j in range(half):
        line_ready(half + j, lambda j=j: v.expand_kept[j] + v.expand_got[j].astype(F32))
    line_step()

    def lay_out(center, store):
        ahead = jnp.concatenate([center[tall - 1 :], center[: tall - 1]], axis=0)
        back = jnp.concatenate([center[1:], center[:1]], axis=0)
        shifts = (
            jnp.where(not_first[:, :share], ahead, 0.0).astype(BF16),
            center.astype(BF16),
            jnp.where(not_last[:, :share], back, 0.0).astype(BF16),
        )
        for tap in range(9):
            begin = tap // 3 * grid_cols
            store(pl.ds(tap * share, share), shifts[tap % 3][begin : begin + local])
        store(pl.ds(taps, wide_taps - taps), jnp.zeros((local, wide_taps - taps), BF16))

    arrived(cells_sent)
    for slot in range(half):
        over = jnp.where(row > 0, v.above_got[slot].astype(F32), 0.0)
        under = jnp.where(row < rows - 1, v.below_got[slot].astype(F32), 0.0)
        center = jnp.concatenate([over, v.cells_got[slot].astype(F32), under], axis=0)
        sides = (center[:, :share], center[:, share:])
        v.cells_pair[slot] = jnp.where(core == 0, sides[1], sides[0]).astype(BF16)
        for side in range(2):

            def store(lanes, value):
                v.window[side, slot, :, lanes] = value

            lay_out(sides[side], store)
        if slot % 2:
            line_step()
    cells_pair = start(pair("cells", 0, v.cells_pair, v.cells_other))

    def norm_back(hat, scale, gain, grad):
        inside = grad * gain
        mean = jnp.mean(inside, axis=-1, keepdims=True)
        along = jnp.mean(inside * hat, axis=-1, keepdims=True)
        return scale * (inside - mean - hat * along)

    arrived(normed_two_back)
    normed_two_grad = jnp.sum(v.normed_two_got[...].astype(F32), axis=0)
    hat, scale = normal(v.after_attend[...])
    v.norm_here[pl.ds(2, 1), :] = jnp.sum(normed_two_grad * hat, axis=0, keepdims=True)
    v.norm_here[pl.ds(3, 1), :] = jnp.sum(normed_two_grad, axis=0, keepdims=True)
    attend_part = norm_back(hat, scale, v.gains[2:3], normed_two_grad)
    attend_grad = v.down_in[0].astype(F32) + attend_part
    v.attend_grad[...] = attend_grad
    branch_in = attend_grad.astype(BF16)
    attended_grad = dot_right(branch_in, v.merge_all[...]).astype(BF16)
    for there in range(rows):
        begin = there * head_part
        v.attended_grad_send[there] = attended_grad[:, begin : begin + head_part]
    v.attended_grad_got[row] = v.attended_grad_send[row]
    attended_back = to_rows(
        "attended_grad",
        lambda there: v.attended_grad_send.at[there],
        v.attended_grad_got.at[row],
    )
    grads_pair.wait_recv()
    cells_pair.wait_recv()
    for slot in range(half):

        def store(lanes, value):
            v.window_other[slot, :, lanes] = value

        lay_out(v.cells_other[slot].astype(F32), store)
    line_step()

    for group in range(0, 9, 4):
        begin, end = group * share, min((group + 4) * share, wide_taps)
        lanes = pl.ds(begin, end - begin)
        mine = v.window[core, :, :, lanes].reshape(half * local, end - begin)
        other = v.window_other[:, :, lanes].reshape(half * local, end - begin)
        whole = dot_left(mine, flat(v.grads_all)) + dot_left(other, flat(v.grads_other))
        for tap in range(group, min(group + 4, 9)):
            at_tap = (tap - group) * share
            v.kernel_kept[tap] = whole[at_tap : at_tap + share]
            line_ready(2 * half + tap, lambda tap=tap: v.kernel_kept[tap])
        line_step()
    merge_kept, merge_send, merge_got = (
        ref.at[:, pl.ds(0, share)] for ref in (v.slope, v.hidden_grad, v.active)
    )
    heads_kept = (slice(None), slice(None), pl.ds(0, 3 * head_part))
    split(dot_in(v.attended_turned[...], branch_in), merge_kept, merge_send)
    merge_pair = start(pair("merge_back", 0, merge_send, merge_got))
    line_step()
    merge_pair.wait_recv()
    gone([merge_pair])
    merge_send[...] = (merge_kept[...] + merge_got[...].astype(F32)).astype(BF16)
    v.merge_pieces[quad] = merge_send[quad]
    merge_back = to_chips(
        "merge_back",
        lambda there: merge_send.at[there],
        lambda step: v.merge_pieces.at[quad],
    )
    arrived(attended_back)
    for head in range(heads_here):
        lanes = pl.ds(head * HEAD_DIM, HEAD_DIM)
        queries, keys, values = (part_of(v.projected, part, head) for part in range(3))
        branch = v.attended_grad_got[:, :, lanes].reshape(length, HEAD_DIM)
        query_grads = []
        for piece in range(rows):
            inside = pl.ds(piece * local, local)
            probs = v.probs[head, inside, :]
            prob_grad = dot_right(branch[piece * local : (piece + 1) * local], values)
            inner_sum = jnp.sum(probs * prob_grad, axis=-1, keepdims=True)
            scored = (probs * (prob_grad - inner_sum)).astype(BF16)
            v.score_grad[inside, :] = scored
            query_grads.append(0.125 * dot_in(scored, keys))
        query_grad = jnp.concatenate(query_grads, axis=0)
        key_grad = 0.125 * dot_left(queries, v.score_grad[...]).T
        value_grad = dot_left(branch, v.probs[head].astype(BF16)).T
        for part, value in enumerate((query_grad, key_grad, value_grad)):
            into = pl.ds(part * head_part + head * HEAD_DIM, HEAD_DIM)
            v.projected_grad[:, into] = value.astype(BF16)
        line_step(2)

    gone(normed_two_back)

    def along(for_end, for_middle):
        return turn(row, toward * jnp.where(is_end, for_end, for_middle), 2 * rows) % rows

    far, over, near = along(3, 2), along(2, 1), along(1, -1)

    def normed_piece(there):
        inside = pl.ds(pl.multiple_of(there * local, local), local)
        v.normed_two_send[there] = dot_right(v.projected_grad[inside, :], v.heads_all[...]).astype(
            BF16
        )

    def normed_in(index, there):
        src, dst = v.normed_two_send.at[there], v.patches_all.at[index]
        return link("normed_in", index, src, dst, inner)

    def normed_over(index, there):
        src, dst = v.normed_two_send.at[there], v.normed_two_got.at[index]
        return link("normed_over", index, src, dst, inner)

    def normed_out():
        src, dst = v.normed_two_send.at[near], v.patches_all.at[rows - 1]
        return link("normed_out", 0, src, dst, outer)

    for index, there in enumerate((far, over, near)):
        normed_piece(there)

        @pl.when(is_end)
        def _():
            normed_in(index, there).start()

    normed_piece(row)

    def normed_across():
        @pl.when(is_middle)
        def _():
            for index, there in enumerate((far, over)):
                normed_in(index, there).wait_recv()
                total = v.normed_two_send[there].astype(F32) + v.patches_all[index].astype(F32)
                v.normed_two_send[there] = total.astype(BF16)
                normed_over(index, there).start()

    def normed_outward():
        @pl.when(is_middle)
        def _():
            normed_over(0, far).wait_recv()
            total = v.normed_two_send[near].astype(F32) + v.normed_two_got[0].astype(F32)
            v.normed_two_send[near] = total.astype(BF16)
            normed_out().start()

    assert done_in[0] >= 2 * half
    split(dot_in(v.normed_turned[...], v.projected_grad[...]), v.expand_kept, v.heads_send, heads_kept[2])
    heads_pair = start(pair("heads_back", 0, v.heads_send, v.heads_got))
    normed_across()
    line_step()
    heads_pair.wait_recv()
    gone([heads_pair])
    v.heads_send[...] = (v.expand_kept[heads_kept] + v.heads_got[...].astype(F32)).astype(BF16)
    v.heads_pieces[quad] = v.heads_send[quad]
    heads_back = to_chips(
        "heads_back",
        lambda there: v.heads_send.at[there],
        lambda step: v.heads_pieces.at[quad],
    )
    line_step()
    normed_outward()

    assert done_over[0] >= 2 * half

    @pl.when(is_end)
    def _():
        for j in range(half, 2 * half):
            line_outward(j).wait_recv()

    v.expand_pieces[quad] = v.expand_sum[quad]
    expand_back = to_chips(
        "expand_back",
        lambda there: v.expand_sum.at[there],
        lambda step: v.expand_pieces.at[quad],
    )

    gone(feed_sent)
    for first in range(0, half, 2):
        cells = v.window[:, pl.ds(first, 2)].reshape(2, 2 * local, wide_taps)
        whole = dot_in(cells[0], v.kernel_all[0]) + dot_in(cells[1], v.kernel_all[1])
        place_in(v.feed_send, first, first + 2, whole.astype(BF16))
        line_step()
    pixels_sent = send_back("pixels", v.feed_send, v.feed_got)

    arrived(merge_back)
    line_ready(chunks - 1, lambda: jnp.sum(v.merge_pieces[...].astype(F32), axis=0))
    arrived(heads_back)
    v.heads_rows[row] = jnp.sum(v.heads_pieces[...].astype(F32), axis=0).astype(BF16)
    heads_rows = to_rows("heads_rows", lambda there: v.heads_rows.at[row], v.heads_rows.at[row])
    line_step()

    own_part = v.normed_two_send[row].astype(F32)

    @pl.when(is_end)
    def _():
        normed_out().wait_recv()
        v.after_attend[...] = own_part + v.patches_all[rows - 1].astype(F32)

    @pl.when(is_middle)
    def _():
        normed_in(2, near).wait_recv()
        normed_over(1, over).wait_recv()
        others = v.patches_all[2].astype(F32) + v.normed_two_got[1].astype(F32)
        v.after_attend[...] = own_part + others

    normed_grad = v.after_attend[...]
    hat, scale = normal(v.patches[...].astype(F32))
    v.attend_grad[...] += norm_back(hat, scale, v.gains[0:1], normed_grad)
    saved = [fetch(6 + half, v.attend_grad, v.patch_gradient)]
    v.norm_here[pl.ds(0, 1), :] = jnp.sum(normed_grad * hat, axis=0, keepdims=True)
    v.norm_here[pl.ds(1, 1), :] = jnp.sum(normed_grad, axis=0, keepdims=True)
    v.norm_send[...] = jnp.zeros_like(v.norm_send)
    for there in range(team):
        lanes = pl.ds(there * share, share)
        v.norm_send[there, pl.ds(0, 4), pl.ds(0, share)] = v.norm_here[pl.ds(0, 4), lanes]
    v.norm_back[at] = v.norm_send[at]
    norm_back_sent = []
    for step in range(1, team):
        there = turn(at, step, team)
        made = link("norm_back", step, v.norm_send.at[there], v.norm_back.at[at], on_team(step))
        norm_back_sent.append(start(made))
    line_step()
    arrived(norm_back_sent)
    v.norm_rows[row] = jnp.sum(v.norm_back[...], axis=0)
    norm_rows = to_rows("norm_rows", lambda there: v.norm_rows.at[row], v.norm_rows.at[row])

    while done_over[0] < chunks:
        line_step()

    arrived(pixels_sent)
    v.pixels_here[...] = jnp.sum(v.feed_got[...].astype(F32), axis=0).astype(BF16)
    saved.append(fetch(7 + half, v.pixels_here, v.pixels))
    arrived(expand_back)
    for chip in range(half):
        columns = pl.ds(chip * width, width)
        saved.append(fetch(8 + half + chip, v.expand_pieces.at[chip], v.expand_out.at[:, columns]))

    @pl.when(is_end)
    def _():
        for j in range(chunks):
            if not half <= j < 2 * half:
                line_outward(j).wait_recv()

    saved.append(fetch(8 + 2 * half, v.shrink_here, v.shrink_out))
    saved.append(fetch(9 + 2 * half, v.kernel_here, v.kernel_out))
    saved.append(fetch(10 + 2 * half, v.merge_here, v.merge_out))
    arrived(heads_rows)
    for there in range(rows):
        for part in range(3):
            into = pl.ds(part * width + there * head_part, head_part)
            v.heads_here[:, into] = v.heads_rows[there, :, pl.ds(part * head_part, head_part)]
    saved.append(fetch(11 + 2 * half, v.heads_here, v.heads_out))
    arrived(norm_rows)
    v.norm_out[...] = jnp.sum(v.norm_rows[...], axis=0)
    for each in started:
        each.wait_send()

    @pl.when(is_end)
    def _():
        for index, there in enumerate((far, over, near)):
            normed_in(index, there).wait_send()
        for j in range(chunks):
            line_inward(j).wait_send()

    @pl.when(is_middle)
    def _():
        for index, there in enumerate((far, over)):
            normed_over(index, there).wait_send()
        normed_out().wait_send()
        for j in range(chunks):
            line_over(j).wait_send()
            line_outward(j).wait_send()

    for each in saved:
        each.wait()


def layer(given, rows, half, share, grid_cols, heads_here, collective_id):
    local, width = given["patches"].shape
    length = rows * local
    block = width // half
    head_part = width // rows
    ff_part = FF // half
    own_rows = half * share
    team = 2 * half
    chunks = 2 * half + 10
    tall = local + 2 * grid_cols
    wide_taps = -(-9 * share // 128) * 128
    vmem = pl.BlockSpec(memory_space=pltpu.VMEM)

    def low(*shape):
        return pltpu.VMEM(shape, BF16)

    def wide(*shape):
        return pltpu.VMEM(shape, F32)

    def out(dtype, *shape):
        return jax.ShapeDtypeStruct(shape, dtype)

    results = dict(
        pixels=out(BF16, local, width),
        patch_gradient=out(F32, local, width),
        heads_out=out(BF16, share, 3 * width),
        merge_out=out(BF16, share, width),
        expand_out=out(BF16, share, FF),
        shrink_out=out(BF16, own_rows, width),
        kernel_out=out(BF16, 9, share, width),
        norm_out=out(F32, 8, 128),
    )
    piece = (half, local, width)
    back = (half, share, width)
    heads_back = (half, share, 3 * head_part)
    line = (chunks, share, width)
    scratch = dict(
        patches_all=low(rows, local, width),
        norm_low=wide(8, 128),
        heads_low=low(share, 3 * head_part),
        heads_all=low(width, 3 * head_part),
        norm_got=wide(team, 8, 128),
        gains=wide(8, width),
        grads_all=low(*piece),
        usable=low(local, 128),
        key_valid=wide(1, length),
        usable_all=low(half, local, 128),
        merge_low=low(share, width),
        merge_all=low(width, width),
        expand_all=low(width, ff_part),
        kernel_all=low(2, wide_taps, width),
        grads_other=low(*piece),
        shrink_all=low(ff_part, width),
        normed=low(length, width),
        normed_turned=low(width, length),
        attended_turned=low(width, local),
        projected=low(length, 3 * head_part),
        probs=wide(heads_here, length, length),
        attended_send=low(rows, local, head_part),
        attended_got=low(rows, local, head_part),
        attended=low(local, width),
        rim_up_send=low(half, grid_cols, block),
        rim_down_send=low(half, grid_cols, block),
        rim_above=low(half, grid_cols, block),
        rim_below=low(half, grid_cols, block),
        feed_part=wide(half, local, block),
        after_attend=wide(local, width),
        normed_two=low(*piece),
        down_got=low(half, half, local, block),
        down_in=low(*piece),
        slope=wide(half, local, ff_part),
        active=low(half, local, ff_part),
        hidden_grad=low(half, local, ff_part),
        feed_send=low(*piece),
        feed_got=low(*piece),
        normed_two_send=low(*piece),
        normed_two_got=low(*piece),
        grad=wide(ff_part, width),
        shrink_send=low(own_rows, width),
        shrink_got=low(own_rows, width),
        expand_kept=wide(half, share, ff_part),
        expand_send=low(half, share, ff_part),
        expand_got=low(half, share, ff_part),
        expand_sum=low(half, share, ff_part),
        expand_pieces=low(half, share, ff_part),
        cells_send=low(half, local, block),
        cells_got=low(half, local, block),
        above_got=low(half, grid_cols, block),
        below_got=low(half, grid_cols, block),
        norm_here=wide(8, width),
        attend_grad=wide(local, width),
        attended_grad_send=low(rows, local, head_part),
        attended_grad_got=low(rows, local, head_part),
        merge_pieces=low(*back),
        window=low(2, half, local, wide_taps),
        window_other=low(half, local, wide_taps),
        cells_pair=low(half, tall, share),
        cells_other=low(half, tall, share),
        kernel_kept=wide(9, share, width),
        score_grad=low(length, length),
        projected_grad=low(length, 3 * head_part),
        heads_send=low(*heads_back),
        heads_got=low(*heads_back),
        heads_pieces=low(*heads_back),
        heads_rows=low(rows, share, 3 * head_part),
        norm_send=wide(team, 8, 128),
        norm_back=wide(team, 8, 128),
        norm_rows=wide(rows, 8, 128),
        line_got=low(*line),
        send_sem=pltpu.SemaphoreType.DMA((len(KINDS), team)),
        recv_sem=pltpu.SemaphoreType.DMA((len(KINDS), team)),
        pair_send=pltpu.SemaphoreType.DMA((len(PAIRS), 9)),
        pair_recv=pltpu.SemaphoreType.DMA((len(PAIRS), 9)),
        line_send=pltpu.SemaphoreType.DMA((3, chunks)),
        own_sem=pltpu.SemaphoreType.DMA((12 + 2 * half,)),
        pixels_here=low(local, width),
        heads_here=low(share, 3 * width),
        merge_here=low(share, width),
        shrink_here=low(own_rows, width),
        kernel_here=low(9, share, width),
        line_recv=pltpu.SemaphoreType.DMA((3, chunks)),
    )
    outside = ("heads", "merge", "expand", "shrink", "kernel")
    names = tuple(given) + tuple(results) + tuple(scratch)
    values = pl.pallas_call(
        functools.partial(layer_body, (rows, half, share, grid_cols, heads_here), names),
        out_shape=list(results.values()),
        in_specs=[
            pl.BlockSpec(memory_space=pl.ANY)
            if name in outside
            else pl.BlockSpec(memory_space=pltpu.SMEM)
            if name == "widths"
            else vmem
            for name in given
        ],
        out_specs=[
            vmem if name == "norm_out" else pl.BlockSpec(memory_space=pl.ANY) for name in results
        ],
        scratch_shapes=list(scratch.values()),
        compiler_params=pltpu.CompilerParams(
            collective_id=collective_id, has_side_effects=True, vmem_limit_bytes=62 << 20
        ),
        cost_estimate=pl.CostEstimate(
            flops=75 * local * width * width,
            bytes_accessed=16 << 20,
            transcendentals=heads_here * length * length,
        ),
        name="layer",
    )(*given.values())
    return dict(zip(results, values))


def per_device(
    patches,
    pixel_grads,
    widths,
    patch_mask,
    heads_weight,
    heads_first,
    heads_second,
    merge_weight,
    merge_first,
    merge_second,
    expand_weight,
    expand_first,
    expand_second,
    shrink_weight,
    shrink_first,
    shrink_second,
    kernel_weight,
    kernel_first,
    kernel_second,
    norm_table,
    norm_first,
    norm_second,
):
    images, grid_rows, grid_cols, width = patches.shape
    rows, cols = lax.axis_size("row"), TEAM
    teams = lax.axis_size("col") // TEAM
    half = cols // 2
    local = images * grid_rows * grid_cols
    share = width // cols
    heads_here = HEADS // rows

    places = [[at * teams + team for team in range(teams)] for at in range(TEAM)]

    def joined(array, axis):
        if teams == 1:
            return array
        return lax.all_gather(array, "col", axis_index_groups=places, axis=axis, tiled=True)

    def scattered(array, axis):
        if teams == 1:
            return array
        return lax.psum_scatter(
            array, "col", axis_index_groups=places, scatter_dimension=axis, tiled=True
        )

    def held(array, axis):
        return array if teams == 1 else joined(array.astype(BF16), axis).astype(F32)

    found = layer(
        dict(
            patches=patches.reshape(local, width),
            grads=pixel_grads.reshape(local, width),
            heads=held(heads_weight, 0),
            norm_table=held(norm_table, 1),
            widths=widths,
            patch_mask=patch_mask.reshape(patch_mask.shape[1:]),
            merge=held(merge_weight, 0),
            expand=held(expand_weight, 0),
            shrink=held(shrink_weight, 0),
            kernel=held(kernel_weight, 1),
        ),
        rows,
        half,
        share,
        grid_cols,
        heads_here,
        1,
    )
    def share_sum(name, axis):
        return scattered(found[name].astype(F32), axis) if teams > 1 else found[name]

    norm_sum = found["norm_out"]
    if teams > 1:
        norm_sum = scattered(norm_sum[:4, :share], 1)
        norm_sum = jnp.pad(norm_sum, ((0, 4), (0, -norm_sum.shape[1] % 128)))
    values = adam_all(
        [
            (share_sum("heads_out", 0), heads_weight, heads_first, heads_second),
            (share_sum("merge_out", 0), merge_weight, merge_first, merge_second),
            (share_sum("expand_out", 0), expand_weight, expand_first, expand_second),
            (share_sum("shrink_out", 0), shrink_weight, shrink_first, shrink_second),
            (share_sum("kernel_out", 1), kernel_weight, kernel_first, kernel_second),
        ],
        (norm_sum, norm_table, norm_first, norm_second),
        (found["pixels"], found["patch_gradient"]),
    )
    *updated, pixels, patch_gradient = values
    return (pixels.reshape(patches.shape), patch_gradient.reshape(patches.shape), *updated)


def solution(mesh):
    tokens_at = P("col", "row", None, None)
    flat_at = P("col", None)
    kernel_at = P(None, "col", None)
    norm_at = P(None, "col")
    return jax.shard_map(
        per_device,
        mesh=mesh,
        in_specs=(tokens_at, tokens_at, P("col"), P("col", None, None))
        + (flat_at,) * 12
        + (kernel_at,) * 3
        + (norm_at,) * 3,
        out_specs=(tokens_at, tokens_at) + (flat_at,) * 20 + (kernel_at,) * 5 + (norm_at,) * 5,
        check_vma=False,
    )
```

time: 1030 us -> 201 us (0.20)
  waiting for transfers between devices: 772 us -> 0 us
  Pallas kernels: 0 us -> 199 us
  matrix products: 107 us -> 0 us
  blocking collectives: 58.3 us -> 0 us
  other arithmetic: 33.9 us -> 0 us
  local copies, waits for them, and re-layouts: 26.6 us -> 0 us
  between operations: 16 us -> 1.51 us
  starting transfers between devices: 10.7 us -> 0 us
    reduce_scatter x7 -> x0, waiting for transfers between devices: 421 us -> none  [the longest x1 141 us: per_device(): lax.psum_scatter(kernel_grad, 'col', scatter_dimension=1, tiled=True)]
    psum x1 -> x0, waiting for transfers between devices: 210 us -> none  [per_device(): lax.psum((partial_shares[0], partial_shares[1], partial_shares[2], partia...]
    pallas_call x0 -> x2, Pallas kernels: none -> 199 us  [the longest x1 178 us: layer(): pl.pallas_call(functools.partial(layer_body, (rows, half, share, grid_col...]
    all_gather x5 -> x0, waiting for transfers between devices: 115 us -> none  [the longest x1 61.8 us: per_device(): lax.all_gather(kernel_weight.astype(jnp.bfloat16), 'col', axis=1, tiled=T...]
    dot_general x45 -> x0, matrix products: 107 us -> none  [the longest x9 17.3 us: per_device(): jnp.einsum('nyxc,nyxd->cd', window, pixel_grads, preferred_element_type=j...]
    all_gather x3 -> x0, blocking collectives: 46.5 us -> none  [the longest x1 19.5 us: per_device(): lax.all_gather(key_part, 'row', axis=1, tiled=True)]
    convert_element_type x16 -> x0, other arithmetic: 27.4 us -> none  [the longest x6 16.7 us: adam_update(): new_master.astype(jnp.bfloat16)]
    unnamed x15 -> x0, waiting for transfers between devices: 21.4 us -> none
  transfers between devices with their start and end apart: 18 -> 0, of which waited for: 14 -> 0; matrix products, arithmetic and copies ran while one was open for 11% -> 0% of each run, Pallas kernels for 0% -> 0%
where the time goes in v1:
time: 201 us; the launch traced here: 200 us
  Pallas kernels  199 us (99%)
    pallas_call x1, Pallas kernels, layer(): pl.pallas_call(functools.partial(layer_body, (rows, half, share, grid_col...  178 us
    pallas_call x1, Pallas kernels, adam_all(): pl.pallas_call(functools.partial(adam_body, plan, (len(params), len(passe...  21.1 us

profile of v1, /device:TPU:0, one launch (start us, length us, event | category | flops | bytes accessed | tf_op | source)
XLA Modules:
  0.0 200.5 jit_solution(8538682731511766322)
XLA Ops:
  1.3 177.9 %layer.1 = (bf16[128,768]{1,0:T(8,128)(2,1)}, f32[128,768]{1,0:T(8,128)}, bf16[96,2304]{1,0:T(8,128)(2,1)}, bf16[96,768]{1,0:T(8,128)(2,1)}, bf16[96,3072]{1,0:T...) custom-call(bf16[128,768]{1,0:T(8,128)(2,1)} %bitcast.6, ...), custom_call_target="tpu_custom_call" | custom-call | flops 5662310400 | bytes 16777216 | tf_op jit(solution)/shard_map/layer/pallas_call | solution.py:1152
  179.3 21.1 %adam.1 = (f32[96,2304]{1,0:T(8,128)}, f32[96,2304]{1,0:T(8,128)}, f32[96,2304]{1,0:T(8,128)}, f32[96,2304]{1,0:T(8,128)}, bf16[96,2304]{1,0:T(8,128)(2,1)}, /*i...) custom-call(bf16[96,2304]{1,0:T(8,128)(2,1)} %get-tuple-element.72.r, ...), custom_call_target="tpu_custom_call" | custom-call | flops 30965760 | bytes 46448640 | tf_op jit(solution)/shard_map/adam/pallas_call | solution.py:137
